TPU v7x, 32 devices: a whole 2x2x4 slice. The times are simulated.
32 devices in a mesh: groups: 2 (over y), row: 4 (over x, core), col: 4 (over z).
Axes of the slice: x: 2, y: 2, z: 4, core: 2. Of those that a mesh axis runs over, the one named last changes fastest.
Arguments:
- basis_values: bfloat16 [4, 4, 2048, 1536], P('row', 'col'), may hold values from -6 to 6
- potential: float32 [4, 4, 2048], P('row', 'col'), may hold values from -0.125 to 0.125
- basis_blocks: int32 [4, 4, 12], P('row', 'col'), may hold values from 0 to 63, as said below
- factor: bfloat16 [16, 4, 128, 1024], P(None, 'row', None, 'col'), may hold values from -0.1875 to 0.1875
Outputs:
- hamiltonian: float32 [32, 4, 16, 4, 128, 128], P('groups', 'row', None, 'col'), parts along dimension 0
- product: float32 [32, 4, 128, 16, 4, 128], P('groups', 'row', None, None, 'col'), parts along dimension 0
There are 2 independent parts, one for each index of `groups`. A program takes and returns all parts, laid end to end along the dimension named above; an argument that names none is the same for every part. Nothing has to cross between parts.
Inputs may be any that keep to these rules, and one draw needn't show every extreme that they name: `basis_blocks`: the 12 blocks of one batch are distinct and lie within 16 consecutive blocks counted cyclically over the 64 blocks of the window; every such range starts at one common offset modulo 16, and every block of the range whose position in it is a multiple of 4 is on the list. Hence at most 16 of a batch's block pairs (I, J) share the same (I mod 4, J mod 4), and some pair of residues has exactly 16.
All inputs are finite; a program needn't handle non-finite values.
Results may differ from a plain program's by a relative error of at most 0.0048.
Values may be sent and summed in bfloat16 or wider, within the bound.
A program may use at most 128 MiB of HBM per device.

v0:
```python
import jax
import jax.numpy as jnp
from jax import lax
from jax.sharding import PartitionSpec as P

NB = 8192
WIN = 16


def from_root(value, axis, source):
    kept = jnp.where(lax.axis_index(axis) == source, value, 0).astype(value.dtype)
    return lax.psum(kept, axis)


def slot_ranks(targets, usable):
    count = targets.shape[0]
    order = jnp.arange(count)
    earlier = order[None, :] < order[:, None]
    same_target = (targets[:, None] == targets[None, :]) & usable[None, :] & earlier
    return jnp.sum(same_target.astype(jnp.int32), axis=1)


def pack_slots(slot_of_item, slot_count, items, labels):
    selector = jnp.arange(slot_count)[:, None] == slot_of_item[None, :]
    packed = jnp.dot(
        selector.astype(jnp.bfloat16), items, preferred_element_type=jnp.float32
    ).astype(jnp.bfloat16)
    slot_labels = jnp.sum(jnp.where(selector, labels[None, :] + 1, 0), axis=1) - 1
    return (packed, slot_labels)


def sum_into_tile(received, received_labels, tile_blocks):
    selector = received_labels[:, None] == jnp.arange(tile_blocks)[None, :]
    return lax.dot_general(
        selector.astype(jnp.bfloat16),
        received,
        (((0,), (0,)), ((), ())),
        preferred_element_type=jnp.float32,
    )


def local(basis_values, potential, basis_blocks, factor):
    row_count = lax.axis_size("row")
    col_count = lax.axis_size("col")
    device_count = row_count * col_count
    phi_batch = basis_values[0, 0]
    weight_batch = potential[0, 0]
    block_list = basis_blocks[0, 0]
    list_length = block_list.shape[0]
    block_size = factor.shape[2]
    block_area = block_size * block_size
    window = WIN
    total_blocks = NB // block_size
    local_rows = total_blocks // row_count
    local_cols = total_blocks // col_count
    tile_blocks = local_rows * local_cols
    weighted = (phi_batch * weight_batch[:, None]).astype(jnp.bfloat16)
    partial_sum = lax.dot_general(
        phi_batch, weighted, (((0,), (0,)), ((), ())), preferred_element_type=jnp.float32
    ).astype(jnp.bfloat16)
    pieces = partial_sum.reshape(list_length, block_size, list_length, block_size).transpose(
        0, 2, 1, 3
    )
    row_share = min(list_length, window // row_count)
    col_share = min(list_length, window // col_count)
    row_label = jnp.broadcast_to(block_list[:, None], (list_length, list_length)).reshape(-1)
    col_label = jnp.broadcast_to(block_list[None, :], (list_length, list_length)).reshape(-1)
    owner = row_label % row_count * col_count + col_label % col_count
    capacity = row_share * col_share
    usable = jnp.ones(owner.shape, bool)
    slot_of_item = owner * capacity + slot_ranks(owner, usable)
    local_label = row_label // row_count * local_cols + col_label // col_count
    packed, slot_labels = pack_slots(
        slot_of_item,
        device_count * capacity,
        pieces.reshape(list_length * list_length, block_area),
        local_label,
    )
    packed = packed.reshape(device_count, capacity, block_area)
    slot_labels = slot_labels.reshape(device_count, capacity)
    received, received_labels = (
        lax.all_to_all(packed, ("row", "col"), split_axis=0, concat_axis=0, tiled=True),
        lax.all_to_all(slot_labels, ("row", "col"), split_axis=0, concat_axis=0, tiled=True),
    )
    tile = sum_into_tile(received.reshape(-1, block_area), received_labels.reshape(-1), tile_blocks)
    tile = tile.reshape(local_rows, local_cols, block_size, block_size)
    hamiltonian = tile.reshape(local_rows, 1, local_cols, 1, block_size, block_size)
    tile_narrow = tile.astype(jnp.bfloat16)
    head_width = factor.shape[3] * col_count
    head_blocks = head_width // block_size
    gathered_rows = []
    for block_row in range(head_blocks):
        gathered_rows.append(
            from_root(tile_narrow[block_row // row_count], "row", block_row % row_count)
        )
    head_stack = jnp.stack(gathered_rows, axis=0)
    head_matrix = head_stack.transpose(0, 2, 1, 3).reshape(head_width, local_cols * block_size)
    piece = lax.all_gather(factor, "col", axis=3, tiled=True)
    width = piece.shape[3]
    product = jnp.dot(
        piece.reshape(local_rows * block_size, width),
        head_matrix,
        preferred_element_type=jnp.float32,
    )
    product = product.reshape(local_rows, 1, block_size, local_cols, 1, block_size)
    return (hamiltonian, product)


def solution(mesh):
    return jax.shard_map(
        local,
        mesh=mesh,
        in_specs=(
            P("row", "col", None, None),
            P("row", "col", None),
            P("row", "col", None),
            P(None, "row", None, "col"),
        ),
        out_specs=(
            P("groups", "row", None, "col", None, None),
            P("groups", "row", None, None, "col", None),
        ),
        check_vma=False,
    )
```

profile of v0, /device:TPU:0, one launch (start us, length us, event | category | flops | bytes accessed | tf_op | source)
XLA Modules:
  0.0 423.9 jit_solution(7756939959881441454)
XLA Ops:
  8.7 0.7 broadcast_in_dim.44
  9.9 0.7 sub.19
  10.6 7.4 %all-to-all-start = ((s32[16,1,16]{2,1,0:T(1,128)}), s32[16,1,16]{2,1,0:T(1,128)S(1)}, u32[]{:S(2)}, u32[]{:S(2)}) async-start(s32[16,1,16]{2,1,0:T(1,128)} %sub.19), calls=%async_computation | async-start | bytes 16384 | tf_op jit(solution)/shard_map/all_to_all | solution.py:83
  18.0 15.6 %fusion = bf16[1536,1536]{0,1:T(8,128)(2,1)} fusion(bf16[1,1,2048,1536]{3,2,1,0:T(8,128)(2,1)} %param.4, f32[2048]{0:T(1024)} %bitcast.89), kind=kOutput, calls=%fused_computation.4 | convolution fusion | flops 9675472896 | bytes 11018240 | tf_op jit(solution)/shard_map/dot_general | solution.py:58
  33.6 6.6 %copy.20 = bf16[1536,1536]{1,0:T(8,128)(2,1)} copy(bf16[1536,1536]{0,1:T(8,128)(2,1)} %fusion) | data formatting | bytes 9437184 | tf_op jit(solution)/shard_map/convert_element_type | solution.py:60
  40.2 9.4 %reshape.287 = bf16[12,128,12,128]{3,2,1,0:T(8,128)(2,1)} reshape(bf16[1536,1536]{1,0:T(8,128)(2,1)} %copy.20) | data formatting | bytes 9437184 | tf_op jit(solution)/shard_map/reshape | solution.py:61
  49.6 4.1 copy.21
  53.8 7.4 %convolution_convert_fusion = bf16[256,16384]{1,0:T(8,128)(2,1)} fusion(bf16[18,8,128,128]{3,2,1,0:T(8,128)(2,1)S(1)} %bitcast.76, s32[144]{0:T(256)S(1)} %multiply_add_fusion), kind=kOutput, calls=%fused_computation | convolution fusion | flops 1212190720 | bytes 13107776 | tf_op jit(solution)/shard_map/dot_general | solution.py:25
  61.2 6.1 %all-to-all-start.1 = ((bf16[16,16,16384]{2,1,0:T(8,128)(2,1)}), bf16[16,16,16384]{2,1,0:T(8,128)(2,1)}, u32[]{:S(2)}, u32[]{:S(2)}) async-start(bf16[16,16,16384]{2,1,0:T(8,128)(2,1)} %bitcast.74), calls=%async_computation.1 | async-start | bytes 16777216 | tf_op jit(solution)/shard_map/all_to_all | solution.py:82
  68.8 182.8 %all-to-all-done.1 = bf16[16,16,16384]{2,1,0:T(8,128)(2,1)} async-done(((bf16[16,16,16384]{2,1,0:T(8,128)(2,1)}), bf16[16,16,16384]{2,1,0:T(8,128)(2,1)}, u32[]{:S(2)}, u32[]{:S(2)}) %all-to-all-start.1) | async-done | bytes 8388640 | tf_op jit(solution)/shard_map/all_to_all | solution.py:82
  251.6 12.0 %fusion.17 = (bf16[256,16384]{1,0:T(8,128)(2,1)S(1)}, f32[256,16384]{1,0:T(8,128)}) fusion(bf16[256,16384]{1,0:T(8,128)(2,1)} %bitcast.7, s32[256]{0:T(256)S(1)} %eq.66), kind=kOutput, calls=%fused_computation.57 | convolution fusion | flops 2151743488 | bytes 33555456 | tf_op jit(solution)/shard_map/dot_general | solution.py:34
  264.0 1.2 copy.29
  265.2 1.2 copy.23
  266.5 1.1 copy.24
  267.7 1.1 copy.27
  269.0 1.1 copy.28
  270.2 1.2 copy.26
  271.4 1.2 copy.22
  272.7 1.1 copy.25
  274.4 14.3 %copy.33 = f32[32,8,128,128]{3,2,1,0:T(8,128)} copy(f32[32,8,128,128]{3,1,2,0:T(8,128)} %bitcast.72) | data formatting | bytes 33554432
  288.8 70.7 %all-reduce.3.cloned.1.call-done = (bf16[1,16,128,128]{3,1,2,0:T(8,128)(2,1)}, bf16[1,16,128,128]{3,1,2,0:T(8,128)(2,1)}, bf16[1,16,128,128]{3,1,2,0:T(8,128)(2,...) async-done(((bf16[1,16,128,128]{3,1,2,0:T(8,128)(2,1)}, ...) | async-done | bytes 4194320 | tf_op jit(solution)/shard_map/psum | solution.py:12
  359.5 2.0 constant_dynamic-update-slice_fusion.7
  361.5 1.9 constant_dynamic-update-slice_fusion.6
  363.3 1.9 constant_dynamic-update-slice_fusion.5
  365.2 1.9 constant_dynamic-update-slice_fusion.4
  367.1 1.9 constant_dynamic-update-slice_fusion.3
  368.9 0.8 constant_dynamic-update-slice_fusion.2
  369.8 0.8 constant_dynamic-update-slice_fusion.1
  370.6 0.8 constant_dynamic-update-slice_fusion
  371.4 12.6 %convolution_bitcast_fusion = f32[256,8,16,128]{3,1,2,0:T(8,128)S(1)} fusion(bf16[2048,1024]{1,0:T(8,128)(2,1)} %bitcast.88, bf16[128,8,16,128]{3,2,1,0:T(8,128)(2,1)} %bitcast.44), kind=kOutput, calls=%fused_computation.2 | convolution fusion | flops 8589934592 | bytes 25165824 | tf_op jit(solution)/shard_map/dot_general | solution.py:100
  384.0 7.5 %copy.43 = f32[256,8,16,128]{3,2,1,0:T(8,128)} copy(f32[256,8,16,128]{3,1,2,0:T(8,128)S(1)} %convolution_bitcast_fusion) | data formatting | bytes 33554432
  391.5 24.9 %copy.31 = f32[16,1,128,16,1,128]{5,4,3,2,1,0:T(1,128)} copy(f32[16,1,128,16,1,128]{2,0,5,3,4,1:T(8,128)} %bitcast.73) | data formatting | bytes 33554432
  (32 shorter events, 4.2 us)
Async XLA Ops:
  10.6 50.6 %all-to-all-start = ((s32[16,1,16]{2,1,0:T(1,128)}), s32[16,1,16]{2,1,0:T(1,128)S(1)}, u32[]{:S(2)}, u32[]{:S(2)}) async-start(s32[16,1,16]{2,1,0:T(1,128)} %sub.19), calls=%async_computation | async-start | bytes 16384 | tf_op jit(solution)/shard_map/all_to_all | solution.py:83
  61.2 190.4 %all-to-all-start.1 = ((bf16[16,16,16384]{2,1,0:T(8,128)(2,1)}), bf16[16,16,16384]{2,1,0:T(8,128)(2,1)}, u32[]{:S(2)}, u32[]{:S(2)}) async-start(bf16[16,16,16384]{2,1,0:T(8,128)(2,1)} %bitcast.74), calls=%async_computation.1 | async-start | bytes 16777216 | tf_op jit(solution)/shard_map/all_to_all | solution.py:82
  67.3 292.2 %all-reduce.3.cloned.1.call-start = ((), (), s32[]{:S(2)}) async-start(), calls=%async_computation.3 | async-start | bytes 8388608 | tf_op jit(solution)/shard_map/psum | solution.py:12
  273.9 97.6 %all-gather.2.cloned.1.call-start = ((), (), s32[]{:S(2)}) async-start(), calls=%async_computation.2 | async-start | bytes 5242880 | tf_op jit(solution)/shard_map/all_gather | solution.py:98
  359.5 9.5 %copy-start.2 = (bf16[1,16,128,128]{3,1,2,0:T(8,128)(2,1)S(1)}, bf16[1,16,128,128]{3,1,2,0:T(8,128)(2,1)}, u32[]{:S(2)}) copy-start(bf16[1,16,128,128]{3,1,2,0:T(8,128)(2,1)} %get-tuple-element.13) | copy-start | bytes 1572868
  359.5 10.3 %copy-start.1 = (bf16[1,16,128,128]{3,1,2,0:T(8,128)(2,1)S(1)}, bf16[1,16,128,128]{3,1,2,0:T(8,128)(2,1)}, u32[]{:S(2)}) copy-start(bf16[1,16,128,128]{3,1,2,0:T(8,128)(2,1)} %get-tuple-element.14) | copy-start | bytes 1572868
  359.5 11.1 %copy-start = (bf16[1,16,128,128]{3,1,2,0:T(8,128)(2,1)S(1)}, bf16[1,16,128,128]{3,1,2,0:T(8,128)(2,1)}, u32[]{:S(2)}) copy-start(bf16[1,16,128,128]{3,1,2,0:T(8,128)(2,1)} %get-tuple-element.15) | copy-start | bytes 1572868
Sparse Core Ops, SparseCore 0:
  274.0 85.4 all-reduce.2
Sparse Core Ops, SparseCore 1:
  275.9 79.1 all-gather.1
where the time goes:
time: 425 us; the launch traced here: 424 us
  waiting for transfers between devices  254 us (60%)
  local copies, waits for them, and re-layouts  91.6 us (22%)
  matrix products  47.6 us (11%)
  between operations  15.6 us (4%)
  starting transfers between devices  13.9 us (3%)
    all_to_all x1, waiting for transfers between devices, local(): lax.all_to_all(packed, ('row', 'col'), split_axis=0, concat_axis=0, tiled...  183 us
    psum x1, waiting for transfers between devices, from_root(): return lax.psum(kept, axis)  70.7 us
    unnamed x24, local copies, waits for them, and re-layouts  58.6 us
    dot_general x1, matrix products, local(): lax.dot_general(phi_batch, weighted, (((0,), (0,)), ((), ())), preferred_...  15.6 us
    dot_general x1, matrix products, local(): jnp.dot(piece.reshape(local_rows * block_size, width), head_matrix, prefe...  12.6 us
    dot_general x1, matrix products, sum_into_tile(): lax.dot_general(selector.astype(jnp.bfloat16), received, (((0,), (0,)), (...  12 us
    another operation x9, local copies, waits for them, and re-layouts, local(): head_stack = jnp.stack(gathered_rows, axis=0)  10 us
    reshape x1, local copies, waits for them, and re-layouts, local(): partial_sum.reshape(list_length, block_size, list_length, block_size)  9.42 us
  transfers between devices with their start and end apart: 4, of which 2 were waited for; matrix products, arithmetic and copies ran while one was open for 17% of the time, Pallas kernels for 0%

commit v1 on v0

v1 whole, which is shorter than its diff:
```python
import functools

import jax
import jax.numpy as jnp
from jax import lax
from jax.experimental import pallas as pl
from jax.experimental.pallas import tpu as pltpu
from jax.sharding import PartitionSpec as P

NB = 8192
WIN = 16
VMEM_LIMIT = 48 * 1024 * 1024


def pack_kernel(half, info, phi_ref, weight_ref, *refs):
    col_refs = refs[:half]
    out_ref, weighted_ref = refs[half:]
    step = pl.program_id(0)
    bs = out_ref.shape[-1]

    @pl.when(step == 0)
    def _():
        out_ref[...] = jnp.zeros_like(out_ref)
        for j in range(half):
            keep = info[half + j].astype(jnp.float32)
            scaled = col_refs[j][...].astype(jnp.float32) * (weight_ref[...] * keep)
            weighted_ref[:, j * bs : (j + 1) * bs] = scaled.astype(jnp.bfloat16)

    total = lax.dot_general(
        phi_ref[...],
        weighted_ref[...],
        (((0,), (0,)), ((), ())),
        preferred_element_type=jnp.float32,
    ).astype(jnp.bfloat16)
    per_step = phi_ref.shape[1] // bs
    for a in range(per_step):
        row_slot = info[3 * half + step * per_step + a]
        for j in range(half):
            out_ref[row_slot + info[2 * half + j]] = total[
                a * bs : (a + 1) * bs, j * bs : (j + 1) * bs
            ]


def sum_kernel(head_rows, head_cols, info, recv_ref, acc_ref, narrow_ref, head_ref):
    step = pl.program_id(0)
    slots = recv_ref.shape[1]

    @pl.when(step == 0)
    def _():
        acc_ref[...] = jnp.zeros_like(acc_ref)

    at = pl.ds(info[head_rows + step] * slots, slots)
    acc_ref[at] += recv_ref[0].astype(jnp.float32)

    @pl.when(step == pl.num_programs(0) - 1)
    def _():
        narrow_ref[...] = acc_ref[...].astype(jnp.bfloat16)
        for i in range(head_rows):
            for t in range(head_cols):
                head_ref[i * head_cols + t] = acc_ref[info[i] * head_cols + t].astype(jnp.bfloat16)


def place_kernel(cols, local_rows, info, acc_ref, out_ref):
    step = pl.program_id(0)
    out_ref[...] = jnp.zeros_like(out_ref)
    base = info[step] * cols
    for t in range(cols):
        out_ref[0, info[local_rows + step * cols + t]] = acc_ref[base + t]


def fill_kernel(cols, local_rows, info, other_ref, tile_ref, out_ref, wide_ref, sems):
    count = other_ref.shape[0]
    wide_ref[...] = other_ref[...].astype(jnp.float32)

    def copy(n):
        i, t = n // cols, n % cols
        return pltpu.make_async_copy(
            wide_ref.at[info[i] * cols + t],
            out_ref.at[i, info[local_rows + n]],
            sems.at[n],
        )

    for n in range(count):
        copy(n).start()
    for n in range(count):
        copy(n).wait()


def product_kernel(head_count, row_count, cols, info, factor_ref, head_ref, out_ref, mat_ref):
    bs = head_ref.shape[-1]
    groups = 2
    width = groups * cols * bs

    @pl.when(pl.program_id(0) == 0)
    def _():
        for i in range(head_count):
            first = info[i] != 0
            for g in range(groups):
                for t in range(cols):
                    block = head_ref[g, i % row_count, (i // row_count) * cols + t]
                    at = (g * cols + t) * bs
                    rows = pl.ds(i * bs, bs)
                    none = jnp.zeros_like(block)
                    mat_ref[rows, at : at + bs] = jnp.where(first, block, none)
                    mat_ref[rows, width + at : width + at + bs] = jnp.where(first, none, block)

    parts = factor_ref.shape[0]
    rows = factor_ref.shape[1] * factor_ref.shape[2]
    left = jnp.concatenate(
        [factor_ref[k].reshape(rows, factor_ref.shape[3]) for k in range(parts)], axis=1
    )
    total = jnp.dot(left, mat_ref[...], preferred_element_type=jnp.float32)
    out_ref[...] = jnp.zeros_like(out_ref)
    local_cols = out_ref.shape[0] // rows
    for n in range(2 * groups * cols):
        out_ref[pl.ds(info[head_count + n], rows, stride=local_cols), :] = total[
            :, n * bs : (n + 1) * bs
        ]


def local(basis_values, potential, basis_blocks, factor):
    row_count = lax.axis_size("row")
    col_count = lax.axis_size("col")
    group = lax.axis_index("groups")
    my_row = lax.axis_index("row")
    my_col = lax.axis_index("col")
    device_count = row_count * col_count
    phi = basis_values[0, 0]
    points, length = phi.shape
    block_list = basis_blocks[0, 0]
    list_length = block_list.shape[0]
    bs = factor.shape[2]
    total_blocks = NB // bs
    local_rows = total_blocks // row_count
    local_cols = total_blocks // col_count
    windows = total_blocks // WIN
    win_rows = WIN // row_count
    win_cols = WIN // col_count
    cols = win_cols // 2
    half = WIN // 2
    slots = win_rows * cols
    head_count = factor.shape[3] * col_count // bs
    params = functools.partial(pltpu.CompilerParams, vmem_limit_bytes=VMEM_LIMIT)

    factors = lax.all_gather(factor[:, 0], "col", axis=0)

    ahead = (block_list[None, :] - block_list[:, None]) % total_blocks
    is_first = jnp.all(ahead < WIN, axis=1)
    start = jnp.sum(jnp.where(is_first, block_list, 0))
    offset = start % WIN
    window = start // WIN
    window_of = lax.all_gather(window[None], ("row", "col"), axis=0, tiled=True)

    position = (block_list - start) % total_blocks
    half_positions = group * half + jnp.arange(half)
    match = position[None, :] == half_positions[:, None]
    list_index = jnp.sum(jnp.where(match, jnp.arange(list_length)[None, :], 0), axis=1)
    present = jnp.any(match, axis=1).astype(jnp.int32)
    col_slot = (offset + half_positions) % col_count * slots + half_positions // col_count % cols
    row_slot = (
        (offset + position) % row_count * (col_count * slots) + position // row_count * cols
    )
    info = jnp.concatenate([list_index, present, col_slot, row_slot]).astype(jnp.int32)

    width = 2 * bs
    packed = pl.pallas_call(
        functools.partial(pack_kernel, half),
        out_shape=jax.ShapeDtypeStruct((device_count * slots, bs, bs), jnp.bfloat16),
        grid_spec=pltpu.PrefetchScalarGridSpec(
            num_scalar_prefetch=1,
            grid=(length // width,),
            in_specs=[
                pl.BlockSpec((points, width), lambda i, info: (0, i)),
                pl.BlockSpec((points, 1), lambda i, info: (0, 0)),
            ]
            + [
                pl.BlockSpec((points, bs), lambda i, info, j=j: (0, info[j]))
                for j in range(half)
            ],
            out_specs=pl.BlockSpec((device_count * slots, bs, bs), lambda i, info: (0, 0, 0)),
            scratch_shapes=[pltpu.VMEM((points, half * bs), jnp.bfloat16)],
        ),
        compiler_params=params(),
    )(info, phi, potential[0, 0][:, None], *([phi] * half))
    received = lax.all_to_all(
        packed.reshape(device_count, slots, bs, bs),
        ("row", "col"),
        split_axis=0,
        concat_axis=0,
        tiled=True,
    )

    rows_held = jnp.arange(local_rows) * row_count + my_row
    relative = (rows_held - offset) % total_blocks
    row_base = relative // WIN * win_rows + relative % WIN // row_count

    def held_cols(of_window, first, count):
        at = (first + jnp.arange(count)) * col_count + (my_col - offset) % col_count
        return (offset + WIN * of_window[:, None] + at[None, :]) % total_blocks // col_count

    row_window = relative // WIN
    own_cols = held_cols(row_window, group * cols, cols).reshape(-1)
    other_cols = held_cols(row_window, (1 - group) * cols, cols).reshape(-1)

    head_rows = max(1, head_count // row_count)
    sum_info = jnp.concatenate([row_base[:head_rows], window_of])
    acc, narrow, head = pl.pallas_call(
        functools.partial(sum_kernel, head_rows, cols),
        out_shape=(
            jax.ShapeDtypeStruct((windows * slots, bs, bs), jnp.float32),
            jax.ShapeDtypeStruct((windows * slots, bs, bs), jnp.bfloat16),
            jax.ShapeDtypeStruct((head_rows * cols, bs, bs), jnp.bfloat16),
        ),
        grid_spec=pltpu.PrefetchScalarGridSpec(
            num_scalar_prefetch=1,
            grid=(device_count,),
            in_specs=[pl.BlockSpec((1, slots, bs, bs), lambda i, info: (i, 0, 0, 0))],
            out_specs=(
                pl.BlockSpec((windows * slots, bs, bs), lambda i, info: (0, 0, 0)),
                pl.BlockSpec((windows * slots, bs, bs), lambda i, info: (0, 0, 0)),
                pl.BlockSpec((head_rows * cols, bs, bs), lambda i, info: (0, 0, 0)),
            ),
        ),
        compiler_params=params(),
    )(sum_info, received)
    heads = lax.all_gather(head, ("groups", "row"), axis=0)
    heads = heads.reshape(2, row_count, head_rows * cols, bs, bs)
    other = lax.ppermute(narrow, "groups", [(0, 1), (1, 0)])

    tile = pl.pallas_call(
        functools.partial(place_kernel, cols, local_rows),
        out_shape=jax.ShapeDtypeStruct((local_rows, local_cols, bs, bs), jnp.float32),
        grid_spec=pltpu.PrefetchScalarGridSpec(
            num_scalar_prefetch=1,
            grid=(local_rows,),
            in_specs=[pl.BlockSpec((windows * slots, bs, bs), lambda i, info: (0, 0, 0))],
            out_specs=pl.BlockSpec((1, local_cols, bs, bs), lambda i, info: (i, 0, 0, 0)),
        ),
        compiler_params=params(),
        cost_estimate=pl.CostEstimate(
            flops=0, bytes_accessed=4 * local_rows * local_cols * bs * bs, transcendentals=0
        ),
    )(jnp.concatenate([row_base, own_cols]), acc)
    tile = pl.pallas_call(
        functools.partial(fill_kernel, cols, local_rows),
        out_shape=jax.ShapeDtypeStruct((local_rows, local_cols, bs, bs), jnp.float32),
        grid_spec=pltpu.PrefetchScalarGridSpec(
            num_scalar_prefetch=1,
            grid=(),
            in_specs=[
                pl.BlockSpec(memory_space=pltpu.VMEM),
                pl.BlockSpec(memory_space=pl.ANY),
            ],
            out_specs=pl.BlockSpec(memory_space=pl.ANY),
            scratch_shapes=[
                pltpu.VMEM((windows * slots, bs, bs), jnp.float32),
                pltpu.SemaphoreType.DMA((windows * slots,)),
            ],
        ),
        input_output_aliases={2: 0},
        compiler_params=params(),
    )(jnp.concatenate([row_base, other_cols]), other, tile)

    head_window = (jnp.arange(head_count) - offset) % total_blocks // WIN
    in_first = (head_window == head_window[0]).astype(jnp.int32)
    pair = jnp.stack([head_window[0], (head_window[0] + 1) % windows])
    product_cols = held_cols(pair, 0, win_cols).reshape(-1)
    chunk = 2
    part_width = factor.shape[3]
    product = pl.pallas_call(
        functools.partial(product_kernel, head_count, row_count, cols),
        out_shape=jax.ShapeDtypeStruct((local_rows * bs * local_cols, bs), jnp.float32),
        grid_spec=pltpu.PrefetchScalarGridSpec(
            num_scalar_prefetch=1,
            grid=(local_rows // chunk,),
            in_specs=[
                pl.BlockSpec((col_count, chunk, bs, part_width), lambda i, info: (0, i, 0, 0)),
                pl.BlockSpec(heads.shape, lambda i, info: (0, 0, 0, 0, 0)),
            ],
            out_specs=pl.BlockSpec((chunk * bs * local_cols, bs), lambda i, info: (i, 0)),
            scratch_shapes=[pltpu.VMEM((head_count * bs, 2 * win_cols * bs), jnp.bfloat16)],
        ),
        compiler_params=params(),
    )(jnp.concatenate([in_first, product_cols]), factors, heads)

    hamiltonian = tile.reshape(local_rows, 1, local_cols, 1, bs, bs)
    return hamiltonian, product.reshape(local_rows, 1, bs, local_cols, 1, bs)


def solution(mesh):
    return jax.shard_map(
        local,
        mesh=mesh,
        in_specs=(
            P("row", "col", None, None),
            P("row", "col", None),
            P("row", "col", None),
            P(None, "row", None, "col"),
        ),
        out_specs=(
            P("groups", "row", None, "col", None, None),
            P("groups", "row", None, None, "col", None),
        ),
        check_vma=False,
    )
```

time: 425 us -> 269 us (0.63)
  waiting for transfers between devices: 254 us -> 19.1 us
  blocking collectives: 0 us -> 162 us
  local copies, waits for them, and re-layouts: 91.6 us -> 9.07 us
  Pallas kernels: 0 us -> 48 us
  matrix products: 47.6 us -> 0 us
  starting transfers between devices: 13.9 us -> 8.99 us
    all_to_all x2 -> x1, waiting for transfers between devices: 183 us -> 0.01 us  [local(): lax.all_to_all(packed.reshape(device_count, slots, bs, bs), ('row', 'col'...]
    unnamed x0 -> x1, blocking collectives: none -> 162 us
    psum x1 -> x0, waiting for transfers between devices: 70.7 us -> none  [from_root(): return lax.psum(kept, axis)]
    unnamed x24 -> x12, local copies, waits for them, and re-layouts: 58.6 us -> 7.76 us
    pallas_call x0 -> x5, Pallas kernels: none -> 48 us  [the longest x1 14.1 us: local(): pl.pallas_call(functools.partial(pack_kernel, half), out_shape=jax.ShapeD...]
    dot_general x4 -> x0, matrix products: 47.6 us -> none  [the longest x1 15.6 us: local(): lax.dot_general(phi_batch, weighted, (((0,), (0,)), ((), ())), preferred_...]
    ppermute x0 -> x1, waiting for transfers between devices: none -> 18.4 us  [local(): other = lax.ppermute(narrow, 'groups', [(0, 1), (1, 0)])]
    reshape x3 -> x0, local copies, waits for them, and re-layouts: 9.59 us -> none  [the longest x1 9.42 us: local(): partial_sum.reshape(list_length, block_size, list_length, block_size)]
  transfers between devices with their start and end apart: 4 -> 4, of which waited for: 2 -> 1; matrix products, arithmetic and copies ran while one was open for 17% -> 1% of each run, Pallas kernels for 0% -> 8%
where the time goes in v1:
time: 269 us
  blocking collectives  162 us (60%)
  Pallas kernels  48 us (18%)
  waiting for transfers between devices  19.1 us (7%)
  between operations  16.9 us (6%)
  local copies, waits for them, and re-layouts  9.07 us (3%)
  starting transfers between devices  8.99 us (3%)
  other arithmetic  4.66 us (2%)
    unnamed x1, blocking collectives  162 us
    ppermute x1, waiting for transfers between devices, local(): other = lax.ppermute(narrow, 'groups', [(0, 1), (1, 0)])  18.4 us
    pallas_call x1, Pallas kernels, local(): pl.pallas_call(functools.partial(pack_kernel, half), out_shape=jax.ShapeD...  14.1 us
    pallas_call x1, Pallas kernels, local(): pl.pallas_call(functools.partial(product_kernel, head_count, row_count, c...  12.7 us
    pallas_call x1, Pallas kernels, local(): pl.pallas_call(functools.partial(sum_kernel, head_rows, cols), out_shape=...  9.68 us
    pallas_call x1, Pallas kernels, local(): pl.pallas_call(functools.partial(place_kernel, cols, local_rows), out_sha...  9.26 us
    unnamed x12, local copies, waits for them, and re-layouts  7.76 us
    all_to_all x1, starting transfers between devices, local(): lax.all_to_all(packed.reshape(device_count, slots, bs, bs), ('row', 'col'...  7.54 us
  transfers between devices with their start and end apart: 4, of which 1 were waited for; matrix products, arithmetic and copies ran while one was open for 1% of the time, Pallas kernels for 8%

profile of v1, /device:TPU:0, one launch (start us, length us, event | category | flops | bytes accessed | tf_op | source)
XLA Modules:
  0.0 268.7 jit_solution(107104865076161790)
XLA Ops:
  7.2 0.9 fusion.2
  8.1 1.3 select_reduce_fusion
  11.3 1.3 fusion.7
  12.7 0.2 compare_reduce_fusion
  12.9 0.2 fusion.3
  13.1 1.1 copy.15.weight_ref
  14.1 0.1 pad_add_fusion.2.info
  14.2 14.1 %shard_map.59 = bf16[128,128,128]{2,1,0:T(8,128)(2,1)S(1)} custom-call(s32[36]{0:T(128)S(1)} %pad_add_fusion.2.info, bf16[2048,1536]{1,0:T(8,128)(2,1)} %bitcast.24, f32[2048,1]{1,0:T(8,128)S(1)} %copy.15.weight_ref, bf16[2048,1536]{1,0:T(8,128)(2,1)} %bitcast.25, bf16[2048,1536]{1,0:T(8,128)(2,1)} %bitcast.26, bf16[2048,1536]{1,0:T(8,128)(2,1)} %bitcast.27, ...), custom_call_target="tpu_custom_call" | custom-call | tf_op jit(solution)/shard_map/pallas_call | solution.py:166
  28.4 2.0 copy-done
  30.4 7.5 %all-to-all-start = ((bf16[16,8,128,128]{3,2,1,0:T(8,128)(2,1)}), bf16[16,8,128,128]{3,2,1,0:T(8,128)(2,1)}, u32[]{:S(2)}, u32[]{:S(2)}) async-start(bf16[16,8,128,128]{3,2,1,0:T(8,128)(2,1)} %bitcast.21), calls=%async_computation | async-start | bytes 8388608 | tf_op jit(solution)/shard_map/all_to_all | solution.py:185
  38.0 0.7 all-gather.5.cloned.1.call-update
  39.4 0.6 dynamic-slice
  40.1 0.7 dynamic-update-slice
  40.8 162.0 %all-reduce = s32[16]{0:T(128)S(1)} all-reduce(s32[16]{0:T(128)S(1)} %dynamic-update-slice), channel_id=1, replica_groups=mesh['groups'=2,'row'=4,'col'=4] {'row','col'}, use_global_device_ids=true, to_apply=%add | all-reduce | flops 16 | bytes 128
  202.8 0.1 pad_add_fusion.1.info
  202.9 9.7 %shard_map.60 = (f32[32,128,128]{2,1,0:T(8,128)S(1)}, bf16[32,128,128]{2,1,0:T(8,128)(2,1)S(1)}, bf16[4,128,128]{2,1,0:T(8,128)(2,1)}) custom-call(s32[18]{0:T(128)S(1)} %pad_add_fusion.1.info, bf16[16,8,128,128]{3,2,1,0:T(8,128)(2,1)} %all-to-all-done.recv_ref), custom_call_target="tpu_custom_call" | custom-call | tf_op jit(solution)/shard_map/pallas_call | solution.py:207
  212.6 1.0 copy-done.3
  213.7 0.1 fusion.17
  213.8 0.1 broadcast_add_fusion
  213.8 1.4 collective-permute-start
  215.2 0.1 broadcast_add_fusion.2
  215.3 0.1 add.274
  215.4 0.1 add.293
  215.5 0.1 add.305
  215.6 0.1 pad_add_fusion.4.info
  215.7 0.1 pad_add_fusion.3
  215.8 9.3 %shard_map.61.tile_ref = f32[16,16,128,128]{3,2,1,0:T(8,128)} custom-call(s32[48]{0:T(128)S(1)} %get-tuple-element.18.info, f32[32,128,128]{2,1,0:T(8,128)S(1)} %get-tuple-element.6.acc_ref), custom_call_target="tpu_custom_call" | custom-call | bytes 16777216 | tf_op jit(solution)/shard_map/pallas_call | solution.py:230
  225.1 18.4 %collective-permute-done.other_ref = bf16[32,128,128]{2,1,0:T(8,128)(2,1)S(1)} collective-permute-done((bf16[32,128,128]{2,1,0:T(8,128)(2,1)}, bf16[32,128,128]{2,1,0:T(8,128)(2,1)S(1)}, u32[]{:S(2)}, u32[]{:S(2)}) %collective-permute-start) | collective-permute-done | bytes 1048608 | tf_op jit(solution)/shard_map/ppermute | solution.py:228
  243.5 2.2 shard_map.62
  245.8 2.2 copy-done.1
  248.0 1.2 copy-done.2
  249.2 12.7 %shard_map.63 = f32[32768,128]{1,0:T(8,128)} custom-call(s32[16]{0:T(128)S(1)} %pad_add_fusion.4.info, bf16[4,16,128,256]{3,2,1,0:T(8,128)(2,1)S(1)} %bitcast.22, bf16[2,4,4,128,128]{4,3,2,1,0:T(8,128)(2,1)S(1)} %bitcast.23), custom_call_target="tpu_custom_call" | custom-call | tf_op jit(solution)/shard_map/pallas_call | solution.py:270
  (24 shorter events, 0.3 us)
Async XLA Ops:
  28.4 2.0 copy-start
  30.4 9.0 %copy-start.4 = (u32[32]{0:T(128)S(1)}, u32[32]{0:T(128)}, u32[]{:S(2)}) copy-start(u32[32]{0:T(128)} %constant.237) | copy-start | bytes 388
  30.4 172.5 %all-to-all-start = ((bf16[16,8,128,128]{3,2,1,0:T(8,128)(2,1)}), bf16[16,8,128,128]{3,2,1,0:T(8,128)(2,1)}, u32[]{:S(2)}, u32[]{:S(2)}) async-start(bf16[16,8,128,128]{3,2,1,0:T(8,128)(2,1)} %bitcast.21), calls=%async_computation | async-start | bytes 8388608 | tf_op jit(solution)/shard_map/all_to_all | solution.py:185
  37.9 207.8 %all-gather.5.cloned.1.call-start = ((), (), s32[]{:S(2)}) async-start(), calls=%async_computation.1 | async-start | bytes 5242880 | tf_op jit(solution)/shard_map/all_gather | solution.py:145
  38.7 207.1 %all-gather.7.cloned.1.call-start = ((), (), s32[]{:S(2)}) async-start(), calls=%async_computation.2 | async-start | bytes 1179648 | tf_op jit(solution)/shard_map/all_gather | solution.py:226
  212.6 1.0 copy-start.3
  213.8 29.6 %collective-permute-start = (bf16[32,128,128]{2,1,0:T(8,128)(2,1)}, bf16[32,128,128]{2,1,0:T(8,128)(2,1)S(1)}, u32[]{:S(2)}, u32[]{:S(2)}) collective-permute-start(bf16[32,128,128]{2,1,0:T(8,128)(2,1)} %copy-done.3), channel_id=1, source_target_pairs={{0,16},{16,0},{1,17},{17,1},{2,18},{18,2},{3,19},{19,3},{4,20},{20... | collective-permute-start | bytes 3145736 | tf_op jit(solution)/shard_map/ppermute | solution.py:228
  245.8 2.2 copy-start.1
  248.0 1.2 copy-start.2
Sparse Core Ops, SparseCore 0:
  40.4 148.9 all-gather.4
  213.7 26.4 all-gather.6

commit v2 on v1

v2 whole, which is shorter than its diff:
```python
import functools

import jax
import jax.numpy as jnp
from jax import lax
from jax.experimental import pallas as pl
from jax.experimental.pallas import tpu as pltpu
from jax.sharding import PartitionSpec as P

NB = 8192
WIN = 16
VMEM_LIMIT = 48 * 1024 * 1024


def pack_kernel(half, extra, info, phi_ref, weight_ref, *refs):
    col_refs = refs[:half]
    out_ref, weighted_ref = refs[half:]
    step = pl.program_id(0)
    bs = out_ref.shape[-1]

    @pl.when(step == 0)
    def _():
        out_ref[...] = jnp.zeros_like(out_ref)
        if extra:
            tag = info[info.shape[0] - 1].astype(jnp.float32)
            out_ref[:, out_ref.shape[1] - extra :, :] = jnp.full(
                (out_ref.shape[0], extra, bs), tag, jnp.float32
            ).astype(jnp.bfloat16)
        for j in range(half):
            keep = info[half + j].astype(jnp.float32)
            scaled = col_refs[j][...].astype(jnp.float32) * (weight_ref[...] * keep)
            weighted_ref[:, j * bs : (j + 1) * bs] = scaled.astype(jnp.bfloat16)

    total = lax.dot_general(
        phi_ref[...],
        weighted_ref[...],
        (((0,), (0,)), ((), ())),
        preferred_element_type=jnp.float32,
    ).astype(jnp.bfloat16)
    per_step = phi_ref.shape[1] // bs
    length = pl.num_programs(0) * per_step
    for a in range(per_step):
        at = step * per_step + a
        device = info[3 * half + at]
        rows = pl.ds(pl.multiple_of(info[3 * half + length + at] * bs, bs), bs)
        for j in range(half):
            out_ref[device + info[2 * half + j], rows, :] = total[
                a * bs : (a + 1) * bs, j * bs : (j + 1) * bs
            ]


def sum_kernel(head_rows, slots, info, recv_ref, *refs):
    acc_ref, narrow_ref, head_ref = refs[-3:]
    step = pl.program_id(0)
    bs = acc_ref.shape[-1]

    @pl.when(step == 0)
    def _():
        acc_ref[...] = jnp.zeros_like(acc_ref)

    sources = recv_ref.shape[0]
    for k in range(sources):
        first = info[head_rows + step * sources + k] * slots
        for n in range(slots):
            acc_ref[first + n] += recv_ref[k, n * bs : (n + 1) * bs, :].astype(jnp.float32)

    @pl.when(step == pl.num_programs(0) - 1)
    def _():
        narrow_ref[...] = acc_ref[...].astype(jnp.bfloat16)
        for i in range(head_rows):
            head_ref[i] = acc_ref[info[i]].astype(jnp.bfloat16)


def place_kernel(local_rows, info, acc_ref, out_ref):
    step = pl.program_id(0)
    out_ref[...] = jnp.zeros_like(out_ref)
    out_ref[0, info[local_rows + step]] = acc_ref[info[step]]


def fill_kernel(narrow_count, wide_count, info, *refs):
    narrow_refs = refs[:narrow_count]
    own_refs = refs[narrow_count : narrow_count + wide_count]
    out_ref, wide_ref, sems = refs[narrow_count + wide_count + 1 :]
    local_rows = out_ref.shape[0]
    for k in range(narrow_count):
        wide_ref[k] = narrow_refs[k][...].astype(jnp.float32)

    def copy(k, i):
        source = wide_ref.at[k] if k < narrow_count else own_refs[k - narrow_count]
        return pltpu.make_async_copy(
            source.at[info[i]],
            out_ref.at[i, info[local_rows * (k + 1) + i]],
            sems.at[k * local_rows + i],
        )

    for k in range(narrow_count + wide_count):
        for i in range(local_rows):
            copy(k, i).start()
    for k in range(narrow_count + wide_count):
        for i in range(local_rows):
            copy(k, i).wait()


def product_kernel(head_count, row_count, cols, info, factor_ref, *refs):
    head_refs = refs[:cols]
    out_ref, mat_ref = refs[cols:]
    bs = out_ref.shape[-1]
    groups = 2
    width = groups * cols * bs

    @pl.when(pl.program_id(0) == 0)
    def _():
        for i in range(head_count):
            first = info[i] != 0
            for g in range(groups):
                for t in range(cols):
                    block = head_refs[t][g, i % row_count, i // row_count]
                    at = (g * cols + t) * bs
                    rows = pl.ds(i * bs, bs)
                    none = jnp.zeros_like(block)
                    mat_ref[rows, at : at + bs] = jnp.where(first, block, none)
                    mat_ref[rows, width + at : width + at + bs] = jnp.where(first, none, block)

    parts = factor_ref.shape[1]
    rows = factor_ref.shape[2] * factor_ref.shape[3]
    left = jnp.concatenate(
        [factor_ref[0, k].reshape(rows, factor_ref.shape[4]) for k in range(parts)], axis=1
    )
    total = jnp.dot(left, mat_ref[...], preferred_element_type=jnp.float32)
    out_ref[...] = jnp.zeros_like(out_ref)
    local_cols = out_ref.shape[0] // rows
    for n in range(2 * groups * cols):
        out_ref[pl.ds(info[head_count + n], rows, stride=local_cols), :] = total[
            :, n * bs : (n + 1) * bs
        ]


def local(basis_values, potential, basis_blocks, factor):
    row_count = lax.axis_size("row")
    col_count = lax.axis_size("col")
    group = lax.axis_index("groups")
    my_row = lax.axis_index("row")
    my_col = lax.axis_index("col")
    device_count = row_count * col_count
    phi = basis_values[0, 0]
    points, length = phi.shape
    block_list = basis_blocks[0, 0]
    list_length = block_list.shape[0]
    bs = factor.shape[2]
    total_blocks = NB // bs
    local_rows = total_blocks // row_count
    local_cols = total_blocks // col_count
    windows = total_blocks // WIN
    win_rows = WIN // row_count
    win_cols = WIN // col_count
    cols = win_cols // 2
    head_count = factor.shape[3] * col_count // bs
    params = functools.partial(pltpu.CompilerParams, vmem_limit_bytes=VMEM_LIMIT)

    half_rows = local_rows // 2
    my_half = lax.dynamic_slice_in_dim(factor[:, 0], group * half_rows, half_rows)
    factors = lax.all_gather(my_half, ("groups", "col"), axis=0)
    factors = factors.reshape(2, col_count, half_rows, bs, factor.shape[3])

    ahead = (block_list[None, :] - block_list[:, None]) % total_blocks
    is_first = jnp.all(ahead < WIN, axis=1)
    start = jnp.sum(jnp.where(is_first, block_list, 0))
    offset = start % WIN
    window = start // WIN

    position = (block_list - start) % total_blocks
    row_device = (offset + position) % row_count * col_count
    row_slot = position // row_count
    width = 2 * bs
    weight = potential[0, 0][:, None]
    received = []
    for t in range(cols):
        chosen = (group * cols + t) * col_count + jnp.arange(col_count)
        match = position[None, :] == chosen[:, None]
        list_index = jnp.sum(jnp.where(match, jnp.arange(list_length)[None, :], 0), axis=1)
        present = jnp.any(match, axis=1).astype(jnp.int32)
        col_device = (offset + chosen) % col_count
        info = jnp.concatenate(
            [list_index, present, col_device, row_device, row_slot, window[None]]
        ).astype(jnp.int32)
        extra = 16 if t == 0 else 0
        packed_shape = (device_count, win_rows * bs + extra, bs)
        packed = pl.pallas_call(
            functools.partial(pack_kernel, col_count, extra),
            out_shape=jax.ShapeDtypeStruct(packed_shape, jnp.bfloat16),
            grid_spec=pltpu.PrefetchScalarGridSpec(
                num_scalar_prefetch=1,
                grid=(length // width,),
                in_specs=[
                    pl.BlockSpec((points, width), lambda i, info: (0, i)),
                    pl.BlockSpec((points, 1), lambda i, info: (0, 0)),
                ]
                + [
                    pl.BlockSpec((points, bs), lambda i, info, j=j: (0, info[j]))
                    for j in range(col_count)
                ],
                out_specs=pl.BlockSpec(packed_shape, lambda i, info: (0, 0, 0)),
                scratch_shapes=[pltpu.VMEM((points, col_count * bs), jnp.bfloat16)],
            ),
            compiler_params=params(),
            cost_estimate=pl.CostEstimate(
                flops=2 * points * length * col_count * bs,
                bytes_accessed=4 * points * length,
                transcendentals=0,
            ),
        )(info, phi, weight, *([phi] * col_count))
        received.append(
            lax.all_to_all(
                packed,
                ("row", "col"),
                split_axis=0,
                concat_axis=0,
                tiled=True,
            )
        )

    rows_held = jnp.arange(local_rows) * row_count + my_row
    relative = (rows_held - offset) % total_blocks
    row_base = relative // WIN * win_rows + relative % WIN // row_count

    def held_cols(of_window, first, count):
        at = (first + jnp.arange(count)) * col_count + (my_col - offset) % col_count
        return (offset + WIN * of_window[:, None] + at[None, :]) % total_blocks // col_count

    row_window = relative // WIN
    head_rows = max(1, head_count // row_count)
    held = windows * win_rows
    window_of = received[0][:, win_rows * bs, 0].astype(jnp.int32)
    sum_info = jnp.concatenate([row_base[:head_rows], window_of])
    own_cols = [held_cols(row_window, group * cols + t, 1).reshape(-1) for t in range(cols)]
    other_cols = [
        held_cols(row_window, (1 - group) * cols + t, 1).reshape(-1) for t in range(cols)
    ]
    accs, heads, others, ahead_of_sum = [], [], [], []
    for t in range(cols):
        acc, narrow, head = pl.pallas_call(
            functools.partial(sum_kernel, head_rows, win_rows),
            out_shape=(
                jax.ShapeDtypeStruct((held, bs, bs), jnp.float32),
                jax.ShapeDtypeStruct((held, bs, bs), jnp.bfloat16),
                jax.ShapeDtypeStruct((head_rows, bs, bs), jnp.bfloat16),
            ),
            grid_spec=pltpu.PrefetchScalarGridSpec(
                num_scalar_prefetch=1,
                grid=(4,),
                in_specs=[
                    pl.BlockSpec(
                        (device_count // 4,) + received[t].shape[1:], lambda i, info: (i, 0, 0)
                    )
                ]
                + [pl.BlockSpec(memory_space=pl.ANY)] * len(ahead_of_sum),
                out_specs=(
                    pl.BlockSpec((held, bs, bs), lambda i, info: (0, 0, 0)),
                    pl.BlockSpec((held, bs, bs), lambda i, info: (0, 0, 0)),
                    pl.BlockSpec((head_rows, bs, bs), lambda i, info: (0, 0, 0)),
                ),
            ),
            compiler_params=params(),
            cost_estimate=pl.CostEstimate(
                flops=0, bytes_accessed=6 * 1024 * held * bs, transcendentals=0
            ),
        )(sum_info, received[t], *ahead_of_sum)
        gathered = lax.all_gather(head, ("groups", "row"), axis=0)
        heads.append(gathered.reshape(2, row_count, head_rows, bs, bs))
        accs.append(acc)
        others.append(lax.ppermute(narrow, "groups", [(0, 1), (1, 0)]))
        if t > 0:
            continue
        tile = pl.pallas_call(
            functools.partial(place_kernel, local_rows),
            out_shape=jax.ShapeDtypeStruct((local_rows, local_cols, bs, bs), jnp.float32),
            grid_spec=pltpu.PrefetchScalarGridSpec(
                num_scalar_prefetch=1,
                grid=(local_rows,),
                in_specs=[pl.BlockSpec((held, bs, bs), lambda i, info: (0, 0, 0))],
                out_specs=pl.BlockSpec((1, local_cols, bs, bs), lambda i, info: (i, 0, 0, 0)),
            ),
            compiler_params=params(),
            cost_estimate=pl.CostEstimate(
                flops=0, bytes_accessed=4 * local_rows * local_cols * bs * bs, transcendentals=0
            ),
        )(jnp.concatenate([row_base, own_cols[0]]), accs[0])
        ahead_of_sum = [tile, gathered, others[0]]

    fills = 2 * cols - 1
    tile = pl.pallas_call(
        functools.partial(fill_kernel, cols, cols - 1),
        out_shape=jax.ShapeDtypeStruct((local_rows, local_cols, bs, bs), jnp.float32),
        grid_spec=pltpu.PrefetchScalarGridSpec(
            num_scalar_prefetch=1,
            grid=(),
            in_specs=[pl.BlockSpec(memory_space=pltpu.VMEM)] * fills
            + [pl.BlockSpec(memory_space=pl.ANY)],
            out_specs=pl.BlockSpec(memory_space=pl.ANY),
            scratch_shapes=[
                pltpu.VMEM((cols, held, bs, bs), jnp.float32),
                pltpu.SemaphoreType.DMA((fills * local_rows,)),
            ],
        ),
        input_output_aliases={fills + 1: 0},
        compiler_params=params(),
    )(jnp.concatenate([row_base] + other_cols + own_cols[1:]), *others, *accs[1:], tile)

    head_window = (jnp.arange(head_count) - offset) % total_blocks // WIN
    in_first = (head_window == head_window[0]).astype(jnp.int32)
    pair = jnp.stack([head_window[0], (head_window[0] + 1) % windows])
    product_cols = held_cols(pair, 0, win_cols).reshape(-1)
    chunk = 2
    part_width = factor.shape[3]
    steps = half_rows // chunk
    product = pl.pallas_call(
        functools.partial(product_kernel, head_count, row_count, cols),
        out_shape=jax.ShapeDtypeStruct((local_rows * bs * local_cols, bs), jnp.float32),
        grid_spec=pltpu.PrefetchScalarGridSpec(
            num_scalar_prefetch=1,
            grid=(local_rows // chunk,),
            in_specs=[
                pl.BlockSpec(
                    (1, col_count, chunk, bs, part_width),
                    lambda i, info: (i // steps, 0, i % steps, 0, 0),
                ),
            ]
            + [pl.BlockSpec(heads[0].shape, lambda i, info: (0, 0, 0, 0, 0))] * cols,
            out_specs=pl.BlockSpec((chunk * bs * local_cols, bs), lambda i, info: (i, 0)),
            scratch_shapes=[pltpu.VMEM((head_count * bs, 2 * win_cols * bs), jnp.bfloat16)],
        ),
        compiler_params=params(),
    )(jnp.concatenate([in_first, product_cols]), factors, *heads)

    hamiltonian = tile.reshape(local_rows, 1, local_cols, 1, bs, bs)
    return hamiltonian, product.reshape(local_rows, 1, bs, local_cols, 1, bs)


def solution(mesh):
    return jax.shard_map(
        local,
        mesh=mesh,
        in_specs=(
            P("row", "col", None, None),
            P("row", "col", None),
            P("row", "col", None),
            P(None, "row", None, "col"),
        ),
        out_specs=(
            P("groups", "row", None, "col", None, None),
            P("groups", "row", None, None, "col", None),
        ),
        check_vma=False,
    )
```

time: 269 us -> 227 us (0.84)
  blocking collectives: 162 us -> 28.9 us
  waiting for transfers between devices: 19.1 us -> 101 us
  starting transfers between devices: 8.99 us -> 15.6 us
    unnamed x1 -> x0, blocking collectives: 162 us -> none
    all_to_all x1 -> x2, waiting for transfers between devices: 0.01 us -> 101 us  [local(): lax.all_to_all(packed, ('row', 'col'), split_axis=0, concat_axis=0, tiled...]
    all_gather x0 -> x2, blocking collectives: none -> 28.9 us  [local(): gathered = lax.all_gather(head, ('groups', 'row'), axis=0)]
    ppermute x1 -> x2, waiting for transfers between devices: 18.4 us -> 0.01 us  [local(): others.append(lax.ppermute(narrow, 'groups', [(0, 1), (1, 0)]))]
    all_to_all x1 -> x2, starting transfers between devices: 7.54 us -> 12.9 us  [local(): lax.all_to_all(packed, ('row', 'col'), split_axis=0, concat_axis=0, tiled...]
    pallas_call x4 -> x6, Pallas kernels: 35.3 us -> 37.3 us  [the longest x2 19.3 us: local(): pl.pallas_call(functools.partial(pack_kernel, col_count, extra), out_shap...]
  transfers between devices with their start and end apart: 4 -> 5, of which waited for: 1 -> 2; matrix products, arithmetic and copies ran while one was open for 1% -> 1% of each run, Pallas kernels for 8% -> 12%
where the time goes in v2:
time: 227 us; the launch traced here: 226 us
  waiting for transfers between devices  101 us (44%)
  Pallas kernels  50.1 us (22%)
  blocking collectives  28.9 us (13%)
  between operations  17 us (7%)
  starting transfers between devices  15.6 us (7%)
  local copies, waits for them, and re-layouts  8.11 us (4%)
  other arithmetic  5.84 us (3%)
    all_to_all x2, waiting for transfers between devices, local(): lax.all_to_all(packed, ('row', 'col'), split_axis=0, concat_axis=0, tiled...  101 us
    all_gather x2, blocking collectives, local(): gathered = lax.all_gather(head, ('groups', 'row'), axis=0)  28.9 us
    pallas_call x2, Pallas kernels, local(): pl.pallas_call(functools.partial(pack_kernel, col_count, extra), out_shap...  19.3 us
    all_to_all x2, starting transfers between devices, local(): lax.all_to_all(packed, ('row', 'col'), split_axis=0, concat_axis=0, tiled...  12.9 us
    pallas_call x1, Pallas kernels, local(): pl.pallas_call(functools.partial(product_kernel, head_count, row_count, c...  12.8 us
    pallas_call x1, Pallas kernels, local(): pl.pallas_call(functools.partial(place_kernel, local_rows), out_shape=jax...  9.23 us
    unnamed x12, local copies, waits for them, and re-layouts  5.92 us
    pallas_call x2, Pallas kernels, local(): pl.pallas_call(functools.partial(sum_kernel, head_rows, win_rows), out_sh...  5.07 us
  transfers between devices with their start and end apart: 5, of which 2 were waited for; matrix products, arithmetic and copies ran while one was open for 1% of the time, Pallas kernels for 12%

profile of v2, /device:TPU:0, one launch (start us, length us, event | category | flops | bytes accessed | tf_op | source)
XLA Modules:
  0.0 226.5 jit_solution(5160345601317479934)
XLA Ops:
  7.2 1.0 fusion.3
  8.1 1.3 select_reduce_fusion
  11.4 1.3 and_select_fusion.7
  12.8 0.2 fusion.5
  13.0 0.2 compare_reduce_fusion
  13.9 1.1 copy.17.weight_ref
  15.0 0.1 concatenate.23.info
  15.1 9.7 %shard_map.59 = bf16[16,528,128]{2,1,0:T(8,128)(2,1)S(1)} custom-call(s32[37]{0:T(128)S(1)} %concatenate.23.info, bf16[2048,1536]{1,0:T(8,128)(2,1)} %bitcast.25, f32[2048,1]{1,0:T(8,128)S(1)} %copy.17.weight_ref, bf16[2048,1536]{1,0:T(8,128)(2,1)} %bitcast.26, bf16[2048,1536]{1,0:T(8,128)(2,1)} %bitcast.27, bf16[2048,1536]{1,0:T(8,128)(2,1)} %bitcast.28, ...), custom_call_target="tpu_custom_call" | custom-call | flops 3221225472 | bytes 12582912 | tf_op jit(solution)/shard_map/pallas_call | solution.py:188
  24.8 1.3 copy-done.1
  26.1 7.4 %all-to-all-start = ((bf16[16,528,128]{2,1,0:T(8,128)(2,1)}), bf16[16,528,128]{2,1,0:T(8,128)(2,1)}, u32[]{:S(2)}, u32[]{:S(2)}) async-start(bf16[16,528,128]{2,1,0:T(8,128)(2,1)} %copy-done.1), calls=%async_computation | async-start | bytes 4325376 | tf_op jit(solution)/shard_map/all_to_all | solution.py:213
  33.6 0.9 constant_dynamic-slice_fusion
  34.5 0.1 concatenate.25.info
  34.6 9.5 %shard_map.61 = bf16[16,512,128]{2,1,0:T(8,128)(2,1)S(1)} custom-call(s32[37]{0:T(128)S(1)} %concatenate.25.info, bf16[2048,1536]{1,0:T(8,128)(2,1)} %bitcast.30, f32[2048,1]{1,0:T(8,128)S(1)} %copy.17.weight_ref, bf16[2048,1536]{1,0:T(8,128)(2,1)} %bitcast.31, bf16[2048,1536]{1,0:T(8,128)(2,1)} %bitcast.32, bf16[2048,1536]{1,0:T(8,128)(2,1)} %bitcast.33, ...), custom_call_target="tpu_custom_call" | custom-call | flops 3221225472 | bytes 12582912 | tf_op jit(solution)/shard_map/pallas_call | solution.py:188
  44.1 1.4 copy-done.2
  45.5 66.0 %all-to-all-done.recv_ref = bf16[16,528,128]{2,1,0:T(8,128)(2,1)} async-done(((bf16[16,528,128]{2,1,0:T(8,128)(2,1)}), bf16[16,528,128]{2,1,0:T(8,128)(2,1)}, u32[]{:S(2)}, u32[]{:S(2)}) %all-to-all-start) | async-done | bytes 2162720 | tf_op jit(solution)/shard_map/all_to_all | solution.py:213
  111.5 5.5 %all-to-all-start.1 = ((bf16[16,512,128]{2,1,0:T(8,128)(2,1)}), bf16[16,512,128]{2,1,0:T(8,128)(2,1)S(1)}, u32[]{:S(2)}, u32[]{:S(2)}) async-start(bf16[16,512,128]{2,1,0:T(8,128)(2,1)} %copy-done.2), calls=%async_computation.1 | async-start | bytes 4194304 | tf_op jit(solution)/shard_map/all_to_all | solution.py:213
  117.2 0.1 fusion.18
  117.4 0.1 add.377
  117.5 1.1 fusion.2
  118.7 4.0 %shard_map.60 = (f32[16,128,128]{2,1,0:T(8,128)S(1)}, bf16[16,128,128]{2,1,0:T(8,128)(2,1)}, bf16[2,128,128]{2,1,0:T(8,128)(2,1)S(1)}) custom-call(s32[18]{0:T(128)S(1)} %pad_add_fusion.1.info, bf16[16,528,128]{2,1,0:T(8,128)(2,1)} %all-to-all-done.recv_ref), custom_call_target="tpu_custom_call" | custom-call | bytes 12582912 | tf_op jit(solution)/shard_map/pallas_call | solution.py:241
  122.7 1.2 collective-permute-start
  124.1 9.2 %shard_map.62.refs_0_.refs_3_ = f32[16,16,128,128]{3,2,1,0:T(8,128)} custom-call(s32[32]{0:T(128)S(1)} %pad_add_fusion.2.info, f32[16,128,128]{2,1,0:T(8,128)S(1)} %get-tuple-element.9.acc_ref), custom_call_target="tpu_custom_call" | custom-call | bytes 16777216 | tf_op jit(solution)/shard_map/pallas_call | solution.py:274
  133.3 12.1 %all-gather = bf16[16,128,128]{2,1,0:T(8,128)(2,1)} all-gather(bf16[2,128,128]{2,1,0:T(8,128)(2,1)S(1)} %get-tuple-element.10), channel_id=2, replica_groups=mesh['groups'=2,'row'=4,'col'=4] {'groups','row'}, dimensions={0}, use_global_device_ids=true | all-gather | bytes 589824 | tf_op jit(solution)/shard_map/all_gather | solution.py:268
  145.4 34.9 %all-to-all-done.1.recv_ref = bf16[16,512,128]{2,1,0:T(8,128)(2,1)S(1)} async-done(((bf16[16,512,128]{2,1,0:T(8,128)(2,1)}), bf16[16,512,128]{2,1,0:T(8,128)(2,1)S(1)}, u32[]{:S(2)}, u32[]{:S(2)}) %all-to-all-start.1) | async-done | bytes 2097184 | tf_op jit(solution)/shard_map/all_to_all | solution.py:213
  180.2 1.0 copy-done.3
  181.3 1.1 shard_map.63
  182.4 1.4 collective-permute-start.1
  183.9 0.1 pad_add_fusion.info
  184.0 16.9 %all-gather.2 = bf16[16,128,128]{2,1,0:T(8,128)(2,1)S(1)} all-gather(bf16[2,128,128]{2,1,0:T(8,128)(2,1)S(1)} %get-tuple-element.13), channel_id=4, replica_groups=mesh['groups'=2,'row'=4,'col'=4] {'groups','row'}, dimensions={0}, use_global_device_ids=true | all-gather | bytes 589824 | tf_op jit(solution)/shard_map/all_gather | solution.py:268
  200.9 3.8 %shard_map.64 = f32[16,16,128,128]{3,2,1,0:T(8,128)} custom-call(s32[64]{0:T(128)S(1)} %pad_add_fusion.info, bf16[16,128,128]{2,1,0:T(8,128)(2,1)} %collective-permute-done.refs_2_.refs_0_, bf16[16,128,128]{2,1,0:T(8,128)(2,1)S(1)} %collective-permute-done.1.refs_1_, f32[16,128,128]{2,1,0:T(8,128)S(1)} %get-tuple-element.12.refs_2_, ...), custom_call_target="tpu_custom_call", output_to_operand_aliasing={{}: (4, {})} | custom-call | tf_op jit(solution)/shard_map/pallas_call | solution.py:291
  204.7 2.2 copy-done.5
  206.9 12.8 %shard_map.65 = f32[32768,128]{1,0:T(8,128)} custom-call(s32[16]{0:T(128)S(1)} %pad_add_fusion.3.info, bf16[2,4,8,128,256]{4,3,2,1,0:T(8,128)(2,1)S(1)} %bitcast.23, bf16[2,4,2,128,128]{4,3,2,1,0:T(8,128)(2,1)S(1)} %bitcast.22, bf16[2,4,2,128,128]{4,3,2,1,0:T(8,128)(2,1)S(1)} %bitcast.24), custom_call_target="tpu_custom_call" | custom-call | tf_op jit(solution)/shard_map/pallas_call | solution.py:316
  (29 shorter events, 0.6 us)
Async XLA Ops:
  7.2 26.4 %copy-start = (bf16[16,1,128,256]{3,2,1,0:T(8,128)(2,1)S(1)}, bf16[16,1,128,256]{3,2,1,0:T(8,128)(2,1)}, u32[]{:S(2)}) copy-start(bf16[16,1,128,256]{3,2,1,0:T(8,128)(2,1)} %param.7) | copy-start | bytes 3145732
  24.8 1.3 copy-start.1
  26.1 85.4 %all-to-all-start = ((bf16[16,528,128]{2,1,0:T(8,128)(2,1)}), bf16[16,528,128]{2,1,0:T(8,128)(2,1)}, u32[]{:S(2)}, u32[]{:S(2)}) async-start(bf16[16,528,128]{2,1,0:T(8,128)(2,1)} %copy-done.1), calls=%async_computation | async-start | bytes 4325376 | tf_op jit(solution)/shard_map/all_to_all | solution.py:213
  33.5 171.1 %all-gather.5.cloned.1.call-start = ((), (), s32[]{:S(2)}) async-start(), calls=%async_computation.2 | async-start | bytes 4718592 | tf_op jit(solution)/shard_map/all_gather | solution.py:162
  44.1 1.4 copy-start.2
  111.5 68.7 %all-to-all-start.1 = ((bf16[16,512,128]{2,1,0:T(8,128)(2,1)}), bf16[16,512,128]{2,1,0:T(8,128)(2,1)S(1)}, u32[]{:S(2)}, u32[]{:S(2)}) async-start(bf16[16,512,128]{2,1,0:T(8,128)(2,1)} %copy-done.2), calls=%async_computation.1 | async-start | bytes 4194304 | tf_op jit(solution)/shard_map/all_to_all | solution.py:213
  122.7 57.5 %collective-permute-start = (bf16[16,128,128]{2,1,0:T(8,128)(2,1)}, bf16[16,128,128]{2,1,0:T(8,128)(2,1)}, u32[]{:S(2)}, u32[]{:S(2)}) collective-permute-start(bf16[16,128,128]{2,1,0:T(8,128)(2,1)} %get-tuple-element.8), channel_id=1, source_target_pairs={{0,16},{16,0},{1,17},{17,1},{2,18},{18,2},{3,19},{19,3},{4,20},{20... | collective-permute-start | bytes 1572872 | tf_op jit(solution)/shard_map/ppermute | solution.py:271
  180.2 1.0 copy-start.3
  182.4 18.5 %collective-permute-start.1 = (bf16[16,128,128]{2,1,0:T(8,128)(2,1)S(1)}, bf16[16,128,128]{2,1,0:T(8,128)(2,1)S(1)}, u32[]{:S(2)}, u32[]{:S(2)}) collective-permute-start(bf16[16,128,128]{2,1,0:T(8,128)(2,1)S(1)} %get-tuple-element.11), channel_id=1, source_target_pairs={{0,16},{16,0},{1,17},{17,1},{2,18},{18,2},{3,19},{19,3},{4,20},{20... | collective-permute-start | bytes 1572872 | tf_op jit(solution)/shard_map/ppermute | solution.py:271
  200.9 3.8 %copy-start.4 = (bf16[16,128,128]{2,1,0:T(8,128)(2,1)S(1)}, bf16[16,128,128]{2,1,0:T(8,128)(2,1)}, u32[]{:S(2)}) copy-start(bf16[16,128,128]{2,1,0:T(8,128)(2,1)} %all-gather) | copy-start | bytes 1572868
  204.7 2.2 copy-start.5
Sparse Core Ops, SparseCore 0:
  36.5 125.8 all-gather.4
